TPU v7x, 32 devices: a whole 2x2x4 slice. The times are simulated.
32 devices in a mesh: ens: 2 (over x), cell: 16 (over z, y, core).
Axes of the slice: x: 2, y: 2, z: 4, core: 2. Of those that a mesh axis runs over, the one named last changes fastest.
Arguments:
- prior_members: float32 [8, 128, 4096], P(None, 'ens', 'cell'), parts along dimension 1, may hold values from -4 to 4
- blocks: bfloat16 [1024, 128, 128], P('cell'), may hold values from -0.3125 to 0.3125
- block_ray: int32 [1024], P('cell'), may hold values from 0 to 15
- block_cell: int32 [1024], P('cell'), may hold values from 0 to 1
- block_count: int32 [16], P('cell'), may hold values from 8 to 64, as said below
- ray_survey: int32 [16], replicated, may hold values from 0 to 7
- observed: float32 [16, 128, 128], P('cell', 'ens'), parts along dimension 1, may hold values from -6 to 6
- noise_scale: float32 [16, 128], P('cell'), may hold values from 0.8 to 1.6
Outputs:
- updated_members: float32 [8, 128, 4096], P(None, 'ens', 'cell'), parts along dimension 1
- last_gradient: bfloat16 [8, 128, 4096], P(None, 'ens', 'cell'), parts along dimension 1
There are 2 independent parts, one for each index of `ens`. A program takes and returns all parts, laid end to end along the dimension named above; an argument that names none is the same for every part. Nothing has to cross between parts.
Inputs may be any that keep to these rules, and one draw needn't show every extreme that they name: `block_count`: slots a slab uses; slots from this count on hold blocks that are not part of the operator. Some slab uses all 64 slots in every draw.
All inputs are finite; a program needn't handle non-finite values.
Results may differ from a plain program's by a relative error of at most 0.0073.
Values may be sent and summed in bfloat16 or wider, within the bound.
No kernel may reach another device: no remote copies, remote signals or barrier semaphores. Data moves between devices by JAX's collectives and lax.ppermute only.
A program may use at most 64 MiB of HBM per device.

v0:
```python
import functools

import jax
import jax.numpy as jnp
from jax import lax
from jax.experimental import pallas as pl
from jax.experimental.pallas import tpu as pltpu
from jax.sharding import PartitionSpec as P

ITERS = 3

ALPHA_PRIOR = 0.5
BETA_TIME = 0.25
GAMMA_DEPTH = 0.25
STEP_SIZE = 0.05
DATA_GAIN = 1.0

SENT_SCALE = 1.0 / 32.0

CHUNK = 8
VMEM_BYTES = 24 * 1024 * 1024
SETUP_VMEM_BYTES = 60 * 1024 * 1024

SMEM = pl.BlockSpec(memory_space=pltpu.SMEM)
VMEM = pl.BlockSpec(memory_space=pltpu.VMEM)
ANY = pl.BlockSpec(memory_space=pl.ANY)
HBM = pl.BlockSpec(memory_space=pltpu.HBM)


class Order:
    def __init__(self, count, ray_blocks):
        self.owned = ray_blocks // count
        self.half_blocks = ray_blocks // 2
        self.upper = count // 4
        self.ring = [chip + side * self.upper for chip in range(self.upper) for side in range(2)]

    def core(self):
        return lax.rem(lax.axis_index("cell"), 2)

    def place(self, core, q):
        owner = lax.div(q, self.owned)
        other_core = lax.rem(owner + core, 2)
        chip = lax.div(owner, 2)
        position = 2 * lax.rem(chip, self.upper) + lax.div(chip, self.upper)
        return other_core * self.half_blocks + position * self.owned + lax.rem(q, self.owned)

    def survey(self, core, survey_ref, i):
        other_core, rest = divmod(i, self.half_blocks)
        position, offset = divmod(rest, self.owned)
        owner = 2 * self.ring[position] + (1 - core if other_core else core)
        return survey_ref[owner * self.owned + offset]


def forward(order, survey_ref, half_ref, dense_ref, own_ref, away_ref):
    core = order.core()
    half = own_ref.shape[0]
    for i in range(2 * half):
        travel = lax.dot_general(
            half_ref[order.survey(core, survey_ref, i)],
            dense_ref[i],
            (((1,), (1,)), ((), ())),
            preferred_element_type=jnp.float32,
        )
        if i < half:
            own_ref[i] = travel
        else:
            away_ref[i - half] = travel


def setup_kernel(
    order, count_ref, ray_hbm, cell_hbm, survey_hbm, members_hbm, blocks_hbm,
    dense_ref, half_ref, own_ref, away_ref,
    ray_ref, cell_ref, survey_ref, members_ref, staged, total, small_sems, sems,
):
    slots, rays, width = blocks_hbm.shape
    chunks = slots // CHUNK
    core = order.core()
    small = [
        pltpu.make_async_copy(source, target, small_sems.at[i])
        for i, (source, target) in enumerate(
            (
                (ray_hbm, ray_ref),
                (cell_hbm, cell_ref),
                (survey_hbm, survey_ref),
                (members_hbm, members_ref),
            )
        )
    ]
    large = []
    for i in range(chunks):
        part = pl.ds(i * CHUNK, CHUNK)
        large.append(pltpu.make_async_copy(blocks_hbm.at[part], staged.at[part], sems.at[i]))
    for copy in small + large:
        copy.start()
    total[...] = jnp.zeros_like(total)
    for copy in small:
        copy.wait()
    half_ref[...] = members_ref[...].astype(half_ref.dtype)
    count = count_ref[0]
    spare = dense_ref.shape[0]
    for i in range(chunks):
        large[i].wait()
        for k in range(i * CHUNK, (i + 1) * CHUNK):
            place = jnp.where(k < count, order.place(core, ray_ref[k]), spare)
            b = cell_ref[k]
            total[b, place] = total[b, place] + staged[k].astype(jnp.float32)
    for b in range(total.shape[0]):
        dense_ref[:, :, b * width : (b + 1) * width] = total[b, :spare].astype(dense_ref.dtype)
    forward(order, survey_ref, half_ref, dense_ref, own_ref, away_ref)


def misfit_kernel(travel_ref, observed_ref, noise_ref, token_ref, out_ref):
    del token_ref
    travel = travel_ref[...]
    spread = noise_ref[...][:, None, :]
    scaled = (travel - observed_ref[...]) / spread
    residual = DATA_GAIN * scaled / (spread * (1.0 + scaled * scaled))
    out_ref[...] = jnp.broadcast_to(residual.astype(out_ref.dtype)[None], out_ref.shape)


def arrival_kernel(observed_ref, halo_ref, token_ref):
    del observed_ref, halo_ref
    token_ref[...] = jnp.zeros_like(token_ref)


def gradient_kernel(
    order, survey_ref, residual_ref, dense_ref, members_ref, prior_ref, chip_ref, link_ref, grad_ref
):
    core = order.core()
    products = [
        jnp.dot(residual_ref[i], dense_ref[i], preferred_element_type=jnp.float32)
        for i in range(residual_ref.shape[0])
    ]
    surveys = members_ref.shape[0]
    for s in range(surveys):
        m = members_ref[s]
        value = ALPHA_PRIOR * (m - prior_ref[s])
        if s > 0:
            value = value + BETA_TIME * (m - members_ref[s - 1])
        if s < surveys - 1:
            value = value + BETA_TIME * (m - members_ref[s + 1])
        neighbours = chip_ref[s].astype(jnp.float32) + link_ref[s].astype(jnp.float32)
        grad_ref[s] = value + GAMMA_DEPTH * (2.0 * m - neighbours)
    for i, product in enumerate(products):
        s = order.survey(core, survey_ref, i)
        grad_ref[s] = grad_ref[s] + product


def finish_gradient(order, survey_ref, residual_ref, dense_ref, partial_ref, grad):
    core = order.core()
    half = residual_ref.shape[0]
    products = [
        jnp.dot(residual_ref[i], dense_ref[half + i], preferred_element_type=jnp.float32)
        for i in range(half)
    ]
    grad[...] = partial_ref[...]
    for i, product in enumerate(products):
        s = order.survey(core, survey_ref, half + i)
        grad[s] = grad[s] + product


def step_kernel(
    order, survey_ref, residual_ref, dense_ref, partial_ref, members_ref,
    out_ref, half_ref, own_ref, away_ref,
    grad,
):
    finish_gradient(order, survey_ref, residual_ref, dense_ref, partial_ref, grad)
    updated = members_ref[...] - STEP_SIZE * grad[...]
    out_ref[...] = updated
    half_ref[...] = updated.astype(half_ref.dtype)
    forward(order, survey_ref, half_ref, dense_ref, own_ref, away_ref)


def last_kernel(
    order, survey_ref, residual_ref, dense_ref, partial_ref, members_ref,
    out_ref, gradient_ref,
    grad,
):
    finish_gradient(order, survey_ref, residual_ref, dense_ref, partial_ref, grad)
    out_ref[...] = members_ref[...] - STEP_SIZE * grad[...]
    gradient_ref[...] = grad[...].astype(gradient_ref.dtype)


def shards(
    prior_members, blocks, block_ray, block_cell, block_count, ray_survey, observed, noise_scale
):
    surveys, ensemble, cells_dev = prior_members.shape
    slots, rays, width = blocks.shape
    ray_blocks = ray_survey.shape[0]
    count = lax.axis_size("cell")
    order = Order(count, ray_blocks)
    owned, half_blocks = order.owned, order.half_blocks
    chips = count // 2
    params = pltpu.CompilerParams(vmem_limit_bytes=VMEM_BYTES)

    def bf16(*shape):
        return jax.ShapeDtypeStruct(shape, jnp.bfloat16)

    def f32(*shape):
        return jax.ShapeDtypeStruct(shape, jnp.float32)

    members_f32 = f32(surveys, ensemble, cells_dev)
    members_bf16 = bf16(surveys, ensemble, cells_dev)
    travels = (f32(half_blocks, ensemble, rays),) * 2

    in_hbm = [
        pltpu.with_memory_space_constraint(array, pltpu.HBM)
        for array in (block_ray, block_cell, ray_survey, prior_members, blocks)
    ]
    dense, half, own, away = pl.pallas_call(
        functools.partial(setup_kernel, order),
        out_shape=(bf16(ray_blocks, rays, cells_dev), members_bf16) + travels,
        in_specs=[SMEM] + [HBM] * 5,
        out_specs=(VMEM,) * 4,
        scratch_shapes=[
            pltpu.SMEM(block_ray.shape, jnp.int32),
            pltpu.SMEM(block_cell.shape, jnp.int32),
            pltpu.SMEM(ray_survey.shape, jnp.int32),
            pltpu.VMEM(prior_members.shape, jnp.float32),
            pltpu.VMEM(blocks.shape, blocks.dtype),
            pltpu.VMEM((cells_dev // width, ray_blocks + 1, rays, width), jnp.float32),
            pltpu.SemaphoreType.DMA((4,)),
            pltpu.SemaphoreType.DMA((slots // CHUNK,)),
        ],
        compiler_params=pltpu.CompilerParams(vmem_limit_bytes=VMEM_BYTES),
    )(block_count, *in_hbm)

    chip_pairs = [(i, i ^ 1) for i in range(count)]
    link_pairs = [pair for i in range(1, count - 1, 2) for pair in ((i, i + 1), (i + 1, i))]
    same_core = [[2 * chip + core for chip in order.ring] for core in range(2)]

    def exchange(array):
        return lax.all_to_all(
            array, "cell", split_axis=0, concat_axis=0, axis_index_groups=same_core, tiled=True
        )

    members = prior_members
    for iteration in range(ITERS):
        received = lax.ppermute(away, "cell", chip_pairs)
        chip_halo = lax.ppermute(half, "cell", chip_pairs)
        received, chip_halo = lax.optimization_barrier((received, chip_halo))
        chip_travel = ((own + received) * SENT_SCALE).astype(jnp.float16)
        link_halo = lax.ppermute(half, "cell", link_pairs)
        parts = exchange(chip_travel)
        parts, after_parts = lax.optimization_barrier((parts, observed))
        token = pl.pallas_call(
            arrival_kernel,
            out_shape=f32(8, 128),
            in_specs=[ANY] * 2,
            out_specs=VMEM,
            compiler_params=params,
        )(after_parts, link_halo)
        parts, token = lax.optimization_barrier((parts, token))
        parts = parts.reshape(chips, owned, ensemble, rays).astype(jnp.float32)
        travel = jnp.sum(parts, axis=0) / SENT_SCALE
        copies = pl.pallas_call(
            misfit_kernel,
            out_shape=bf16(chips, owned, ensemble, rays),
            in_specs=[VMEM] * 3 + [ANY],
            out_specs=VMEM,
            compiler_params=params,
        )(travel, observed, noise_scale, token)
        residual = exchange(copies.reshape(half_blocks, ensemble, rays))
        other_residual = lax.ppermute(residual, "cell", chip_pairs)
        partial = pl.pallas_call(
            functools.partial(gradient_kernel, order),
            out_shape=members_f32,
            in_specs=[SMEM] + [VMEM] * 6,
            out_specs=VMEM,
            compiler_params=params,
        )(ray_survey, residual, dense, members, prior_members, chip_halo, link_halo)
        last = iteration == ITERS - 1
        outputs = (members_f32, members_bf16) + (() if last else travels)
        results = pl.pallas_call(
            functools.partial(last_kernel if last else step_kernel, order),
            out_shape=outputs,
            in_specs=[SMEM] + [VMEM] * 4,
            out_specs=(VMEM,) * len(outputs),
            scratch_shapes=[pltpu.VMEM(prior_members.shape, jnp.float32)],
            compiler_params=params,
        )(ray_survey, other_residual, dense, partial, members)
        if last:
            return results
        members, half, own, away = results


def solution(mesh):
    placed = (
        P(None, "ens", "cell"),
        P("cell", None, None),
        P("cell"),
        P("cell"),
        P("cell"),
        P(),
        P("cell", "ens", None),
        P("cell", None),
    )
    return jax.shard_map(
        shards,
        mesh=mesh,
        in_specs=placed,
        out_specs=(P(None, "ens", "cell"), P(None, "ens", "cell")),
        check_vma=False,
    )
```

profile of v0, /device:TPU:0, one launch (start us, length us, event | category | flops | bytes accessed | tf_op | source)
XLA Modules:
  0.0 85.7 jit_solution(14250768319115932067)
XLA Ops:
  1.3 3.0 %shard_map.95 = (bf16[16,128,256]{2,1,0:T(8,128)(2,1)S(1)}, bf16[8,64,256]{2,1,0:T(8,128)(2,1)S(1)}, f32[8,64,128]{2,1,0:T(8,128)S(1)}, f32[8,64,128]{2,1,0:T(8,128)S(1)}) custom-call(s32[1]{0:T(128)S(6)} %copy.10.count_ref, s32[64]{0:T(128)} %ray_hbm.1, s32[64]{0:T(128)} %cell_hbm.1, s32[16]{0:T(128)} %survey_ref.11, f32[8,64,256]{2,1,0:T(8,128)} %prior_ref.5, ...), custom_call_target="tpu_custom_call" | custom-call | tf_op jit(solution)/shard_map/pallas_call | solution.py:210
  4.3 0.5 collective-permute-start
  4.8 0.1 collective-permute-start.1
  4.9 0.7 collective-permute-start.2
  5.6 0.4 collective-permute-done
  6.0 0.4 collective-permute-done.1.chip_ref
  6.4 15.4 %all_to_all.30 = f16[8,64,128]{2,1,0:T(8,128)(2,1)S(1)} all-to-all(f16[8,64,128]{2,1,0:T(8,128)(2,1)S(1)} %multiply_convert_fusion.2), channel_id=1, replica_groups={{0,8,2,10,4,12,6,14},{1,9,3,11,5,13,7,15},{16,24,18,26,20,28,22,30},{17..., dimensions={0} | all-to-all | bytes 262144 | tf_op jit(solution)/shard_map/all_to_all | solution.py:233
  21.9 9.9 %all_to_all.31.residual_ref = bf16[8,64,128]{2,1,0:T(8,128)(2,1)S(1)} all-to-all(bf16[8,64,128]{2,1,0:T(8,128)(2,1)S(1)} %bitcast.9), channel_id=1, replica_groups={{0,8,2,10,4,12,6,14},{1,9,3,11,5,13,7,15},{16,24,18,26,20,28,22,30},{17..., dimensions={0} | all-to-all | bytes 262144 | tf_op jit(solution)/shard_map/all_to_all | solution.py:233
  31.7 1.0 %shard_map.98.partial_ref = f32[8,64,256]{2,1,0:T(8,128)S(1)} custom-call(s32[16]{0:T(128)S(1)} %copy-done.2, bf16[8,64,128]{2,1,0:T(8,128)(2,1)S(1)} %all_to_all.31.residual_ref, bf16[16,128,256]{2,1,0:T(8,128)(2,1)S(1)} %get-tuple-element.40.dense_ref, f32[8,64,256]{2,1,0:T(8,128)S(1)} %copy-done, f32[8,64,256]{2,1,0:T(8,128)S(1)} %copy-done, ...), custom_call_target="tpu_custom_call" | custom-call | tf_op jit(solution)/shard_map/pallas_call | solution.py:265
  32.7 0.4 collective-permute-done.3.residual_ref
  33.1 1.3 %shard_map.99 = (f32[8,64,256]{2,1,0:T(8,128)S(1)}, bf16[8,64,256]{2,1,0:T(8,128)(2,1)S(1)}, f32[8,64,128]{2,1,0:T(8,128)S(1)}, f32[8,64,128]{2,1,0:T(8,128)S(1)}) custom-call(s32[16]{0:T(128)S(1)} %copy-done.2, bf16[8,64,128]{2,1,0:T(8,128)(2,1)S(1)} %collective-permute-done.3.residual_ref, bf16[16,128,256]{2,1,0:T(8,128)(2,1)S(1)} %get-tuple-element.40.dense_ref, ...), custom_call_target="tpu_custom_call" | custom-call | tf_op jit(solution)/shard_map/pallas_call | solution.py:274
  34.4 0.2 collective-permute-start.4
  34.6 0.4 collective-permute-start.5
  35.0 0.7 collective-permute-start.6
  35.6 0.4 collective-permute-done.4
  36.0 0.4 collective-permute-done.5.chip_ref
  36.4 10.9 %all_to_all.32 = f16[8,64,128]{2,1,0:T(8,128)(2,1)S(1)} all-to-all(f16[8,64,128]{2,1,0:T(8,128)(2,1)S(1)} %multiply_convert_fusion.1), channel_id=1, replica_groups={{0,8,2,10,4,12,6,14},{1,9,3,11,5,13,7,15},{16,24,18,26,20,28,22,30},{17..., dimensions={0} | all-to-all | bytes 262144 | tf_op jit(solution)/shard_map/all_to_all | solution.py:233
  47.4 9.8 %all_to_all.33.residual_ref = bf16[8,64,128]{2,1,0:T(8,128)(2,1)S(1)} all-to-all(bf16[8,64,128]{2,1,0:T(8,128)(2,1)S(1)} %bitcast.10), channel_id=1, replica_groups={{0,8,2,10,4,12,6,14},{1,9,3,11,5,13,7,15},{16,24,18,26,20,28,22,30},{17..., dimensions={0} | all-to-all | bytes 262144 | tf_op jit(solution)/shard_map/all_to_all | solution.py:233
  57.2 1.0 %shard_map.102.partial_ref = f32[8,64,256]{2,1,0:T(8,128)S(1)} custom-call(s32[16]{0:T(128)S(1)} %copy-done.2, bf16[8,64,128]{2,1,0:T(8,128)(2,1)S(1)} %all_to_all.33.residual_ref, bf16[16,128,256]{2,1,0:T(8,128)(2,1)S(1)} %get-tuple-element.40.dense_ref, f32[8,64,256]{2,1,0:T(8,128)S(1)} %get-tuple-element.50.members_ref, f32[8,64,256]{2,1,0:T(8,128)S(1)} %copy-done, ...), custom_call_target="tpu_custom_call" | custom-call | tf_op jit(solution)/shard_map/pallas_call | solution.py:265
  58.2 0.4 collective-permute-done.7.residual_ref
  58.5 1.3 %shard_map.103 = (f32[8,64,256]{2,1,0:T(8,128)S(1)}, bf16[8,64,256]{2,1,0:T(8,128)(2,1)S(1)}, f32[8,64,128]{2,1,0:T(8,128)S(1)}, f32[8,64,128]{2,1,0:T(8,128)S(1)}) custom-call(s32[16]{0:T(128)S(1)} %copy-done.2, bf16[8,64,128]{2,1,0:T(8,128)(2,1)S(1)} %collective-permute-done.7.residual_ref, bf16[16,128,256]{2,1,0:T(8,128)(2,1)S(1)} %get-tuple-element.40.dense_ref, ...), custom_call_target="tpu_custom_call" | custom-call | tf_op jit(solution)/shard_map/pallas_call | solution.py:274
  59.9 0.2 collective-permute-start.8
  60.1 0.4 collective-permute-start.9
  60.4 0.7 collective-permute-start.10
  61.1 0.4 collective-permute-done.8
  61.5 0.4 collective-permute-done.9.chip_ref
  61.9 10.9 %all_to_all.34 = f16[8,64,128]{2,1,0:T(8,128)(2,1)S(1)} all-to-all(f16[8,64,128]{2,1,0:T(8,128)(2,1)S(1)} %multiply_convert_fusion), channel_id=1, replica_groups={{0,8,2,10,4,12,6,14},{1,9,3,11,5,13,7,15},{16,24,18,26,20,28,22,30},{17..., dimensions={0} | all-to-all | bytes 262144 | tf_op jit(solution)/shard_map/all_to_all | solution.py:233
  72.9 9.8 %all_to_all.35.residual_ref = bf16[8,64,128]{2,1,0:T(8,128)(2,1)S(1)} all-to-all(bf16[8,64,128]{2,1,0:T(8,128)(2,1)S(1)} %bitcast.11), channel_id=1, replica_groups={{0,8,2,10,4,12,6,14},{1,9,3,11,5,13,7,15},{16,24,18,26,20,28,22,30},{17..., dimensions={0} | all-to-all | bytes 262144 | tf_op jit(solution)/shard_map/all_to_all | solution.py:233
  82.7 0.0 collective-permute-start.11
  82.7 1.0 %shard_map.106.partial_ref = f32[8,64,256]{2,1,0:T(8,128)S(1)} custom-call(s32[16]{0:T(128)S(1)} %copy-done.2, bf16[8,64,128]{2,1,0:T(8,128)(2,1)S(1)} %all_to_all.35.residual_ref, bf16[16,128,256]{2,1,0:T(8,128)(2,1)S(1)} %get-tuple-element.40.dense_ref, f32[8,64,256]{2,1,0:T(8,128)S(1)} %get-tuple-element.60.members_ref, f32[8,64,256]{2,1,0:T(8,128)S(1)} %copy-done, ...), custom_call_target="tpu_custom_call" | custom-call | tf_op jit(solution)/shard_map/pallas_call | solution.py:265
  83.6 0.4 collective-permute-done.11.residual_ref
  84.0 1.7 %shard_map.107 = (f32[8,64,256]{2,1,0:T(8,128)}, bf16[8,64,256]{2,1,0:T(8,128)(2,1)}) custom-call(s32[16]{0:T(128)S(1)} %copy-done.2, bf16[8,64,128]{2,1,0:T(8,128)(2,1)S(1)} %collective-permute-done.11.residual_ref, bf16[16,128,256]{2,1,0:T(8,128)(2,1)S(1)} %get-tuple-element.40.dense_ref, f32[8,64,256]{2,1,0:T(8,128)S(1)} %shard_map.106.partial_ref, ...), custom_call_target="tpu_custom_call" | custom-call | tf_op jit(solution)/shard_map/pallas_call | solution.py:274
  (28 shorter events, 0.3 us)
Async XLA Ops:
  0.6 21.2 %copy-start.1 = (f32[1,64,128]{2,1,0:T(8,128)S(1)}, f32[1,64,128]{2,1,0:T(8,128)}, u32[]{:S(2)}) copy-start(f32[1,64,128]{2,1,0:T(8,128)} %observed_ref.8) | copy-start | bytes 98308
  0.6 21.2 %copy-start.3 = (f32[1,128]{1,0:T(1,128)S(1)}, f32[1,128]{1,0:T(1,128)}, u32[]{:S(2)}) copy-start(f32[1,128]{1,0:T(1,128)} %noise_ref.5) | copy-start | bytes 1540
  1.3 30.4 %copy-start = (f32[8,64,256]{2,1,0:T(8,128)S(1)}, f32[8,64,256]{2,1,0:T(8,128)}, u32[]{:S(2)}) copy-start(f32[8,64,256]{2,1,0:T(8,128)} %prior_ref.5) | copy-start | bytes 1572868
  1.3 30.4 %copy-start.2 = (s32[16]{0:T(128)S(1)}, s32[16]{0:T(128)}, u32[]{:S(2)}) copy-start(s32[16]{0:T(128)} %survey_ref.11) | copy-start | bytes 196
  4.3 1.7 %collective-permute-start = (f32[8,64,128]{2,1,0:T(8,128)S(1)}, f32[8,64,128]{2,1,0:T(8,128)S(1)}, u32[]{:S(2)}, u32[]{:S(2)}) collective-permute-start(f32[8,64,128]{2,1,0:T(8,128)S(1)} %get-tuple-element.33), channel_id=1, source_target_pairs={{0,1},{1,0},{2,3},{3,2},{4,5},{5,4},{6,7},{7,6},{8,9},{9,8},{10,11... | collective-permute-start | bytes 786440 | tf_op jit(solution)/shard_map/ppermute | solution.py:239
  4.8 1.5 %collective-permute-start.1 = (bf16[8,64,256]{2,1,0:T(8,128)(2,1)S(1)}, bf16[8,64,256]{2,1,0:T(8,128)(2,1)S(1)}, u32[]{:S(2)}, u32[]{:S(2)}) collective-permute-start(bf16[8,64,256]{2,1,0:T(8,128)(2,1)S(1)} %get-tuple-element.34), channel_id=1, source_target_pairs={{0,1},{1,0},{2,3},{3,2},{4,5},{5,4},{6,7},{7,6},{8,9},{9,8},{10,11... | collective-permute-start | bytes 786440 | tf_op jit(solution)/shard_map/ppermute | solution.py:240
  4.9 16.9 %collective-permute-start.2 = (bf16[8,64,256]{2,1,0:T(8,128)(2,1)S(1)}, bf16[8,64,256]{2,1,0:T(8,128)(2,1)S(1)}, u32[]{:S(2)}, u32[]{:S(2)}) collective-permute-start(bf16[8,64,256]{2,1,0:T(8,128)(2,1)S(1)} %get-tuple-element.34), channel_id=1, source_target_pairs={{1,2},{2,1},{3,4},{4,3},{5,6},{6,5},{7,8},{8,7},{9,10},{10,9},{11,... | collective-permute-start | bytes 786440 | tf_op jit(solution)/shard_map/ppermute | solution.py:243
  31.7 1.3 %collective-permute-start.3 = (bf16[8,64,128]{2,1,0:T(8,128)(2,1)S(1)}, bf16[8,64,128]{2,1,0:T(8,128)(2,1)S(1)}, u32[]{:S(2)}, u32[]{:S(2)}) collective-permute-start(bf16[8,64,128]{2,1,0:T(8,128)(2,1)S(1)} %all_to_all.31.residual_ref), channel_id=1, source_target_pairs={{0,1},{1,0},{2,3},{3,2},{4,5},{5,4},{6,7},{7,6},{8,9},{9,8},{10,11... | collective-permute-start | bytes 393224 | tf_op jit(solution)/shard_map/ppermute | solution.py:264
  34.4 1.6 %collective-permute-start.4 = (f32[8,64,128]{2,1,0:T(8,128)S(1)}, f32[8,64,128]{2,1,0:T(8,128)S(1)}, u32[]{:S(2)}, u32[]{:S(2)}) collective-permute-start(f32[8,64,128]{2,1,0:T(8,128)S(1)} %get-tuple-element.43), channel_id=1, source_target_pairs={{0,1},{1,0},{2,3},{3,2},{4,5},{5,4},{6,7},{7,6},{8,9},{9,8},{10,11... | collective-permute-start | bytes 786440 | tf_op jit(solution)/shard_map/ppermute | solution.py:239
  34.6 1.8 %collective-permute-start.5 = (bf16[8,64,256]{2,1,0:T(8,128)(2,1)S(1)}, bf16[8,64,256]{2,1,0:T(8,128)(2,1)S(1)}, u32[]{:S(2)}, u32[]{:S(2)}) collective-permute-start(bf16[8,64,256]{2,1,0:T(8,128)(2,1)S(1)} %get-tuple-element.44), channel_id=1, source_target_pairs={{0,1},{1,0},{2,3},{3,2},{4,5},{5,4},{6,7},{7,6},{8,9},{9,8},{10,11... | collective-permute-start | bytes 786440 | tf_op jit(solution)/shard_map/ppermute | solution.py:240
  35.0 12.4 %collective-permute-start.6 = (bf16[8,64,256]{2,1,0:T(8,128)(2,1)S(1)}, bf16[8,64,256]{2,1,0:T(8,128)(2,1)S(1)}, u32[]{:S(2)}, u32[]{:S(2)}) collective-permute-start(bf16[8,64,256]{2,1,0:T(8,128)(2,1)S(1)} %get-tuple-element.44), channel_id=1, source_target_pairs={{1,2},{2,1},{3,4},{4,3},{5,6},{6,5},{7,8},{8,7},{9,10},{10,9},{11,... | collective-permute-start | bytes 786440 | tf_op jit(solution)/shard_map/ppermute | solution.py:243
  57.2 1.3 %collective-permute-start.7 = (bf16[8,64,128]{2,1,0:T(8,128)(2,1)S(1)}, bf16[8,64,128]{2,1,0:T(8,128)(2,1)S(1)}, u32[]{:S(2)}, u32[]{:S(2)}) collective-permute-start(bf16[8,64,128]{2,1,0:T(8,128)(2,1)S(1)} %all_to_all.33.residual_ref), channel_id=1, source_target_pairs={{0,1},{1,0},{2,3},{3,2},{4,5},{5,4},{6,7},{7,6},{8,9},{9,8},{10,11... | collective-permute-start | bytes 393224 | tf_op jit(solution)/shard_map/ppermute | solution.py:264
  59.9 1.6 %collective-permute-start.8 = (f32[8,64,128]{2,1,0:T(8,128)S(1)}, f32[8,64,128]{2,1,0:T(8,128)S(1)}, u32[]{:S(2)}, u32[]{:S(2)}) collective-permute-start(f32[8,64,128]{2,1,0:T(8,128)S(1)} %get-tuple-element.53), channel_id=1, source_target_pairs={{0,1},{1,0},{2,3},{3,2},{4,5},{5,4},{6,7},{7,6},{8,9},{9,8},{10,11... | collective-permute-start | bytes 786440 | tf_op jit(solution)/shard_map/ppermute | solution.py:239
  60.1 1.8 %collective-permute-start.9 = (bf16[8,64,256]{2,1,0:T(8,128)(2,1)S(1)}, bf16[8,64,256]{2,1,0:T(8,128)(2,1)S(1)}, u32[]{:S(2)}, u32[]{:S(2)}) collective-permute-start(bf16[8,64,256]{2,1,0:T(8,128)(2,1)S(1)} %get-tuple-element.54), channel_id=1, source_target_pairs={{0,1},{1,0},{2,3},{3,2},{4,5},{5,4},{6,7},{7,6},{8,9},{9,8},{10,11... | collective-permute-start | bytes 786440 | tf_op jit(solution)/shard_map/ppermute | solution.py:240
  60.4 12.3 %collective-permute-start.10 = (bf16[8,64,256]{2,1,0:T(8,128)(2,1)S(1)}, bf16[8,64,256]{2,1,0:T(8,128)(2,1)S(1)}, u32[]{:S(2)}, u32[]{:S(2)}) collective-permute-start(bf16[8,64,256]{2,1,0:T(8,128)(2,1)S(1)} %get-tuple-element.54), channel_id=1, source_target_pairs={{1,2},{2,1},{3,4},{4,3},{5,6},{6,5},{7,8},{8,7},{9,10},{10,9},{11,... | collective-permute-start | bytes 786440 | tf_op jit(solution)/shard_map/ppermute | solution.py:243
  82.7 1.3 %collective-permute-start.11 = (bf16[8,64,128]{2,1,0:T(8,128)(2,1)S(1)}, bf16[8,64,128]{2,1,0:T(8,128)(2,1)S(1)}, u32[]{:S(2)}, u32[]{:S(2)}) collective-permute-start(bf16[8,64,128]{2,1,0:T(8,128)(2,1)S(1)} %all_to_all.35.residual_ref), channel_id=1, source_target_pairs={{0,1},{1,0},{2,3},{3,2},{4,5},{5,4},{6,7},{7,6},{8,9},{9,8},{10,11... | collective-permute-start | bytes 393224 | tf_op jit(solution)/shard_map/ppermute | solution.py:264
where the time goes:
time: 86.2 us; the launch traced here: 85.7 us
  blocking collectives  66.6 us (77%)
  Pallas kernels  10.3 us (12%)
  starting transfers between devices  3.75 us (4%)
  waiting for transfers between devices  3.37 us (4%)
  between operations  1.49 us (2%)
    all_to_all x6, blocking collectives, exchange(): lax.all_to_all(array, 'cell', split_axis=0, concat_axis=0, axis_index_gro...  66.6 us
    pallas_call x3, Pallas kernels, shards(): pl.pallas_call(functools.partial(last_kernel if last else step_kernel, or...  4.37 us
    pallas_call x1, Pallas kernels, shards(): pl.pallas_call(functools.partial(setup_kernel, order), out_shape=(bf16(ra...  2.98 us
    pallas_call x3, Pallas kernels, shards(): pl.pallas_call(functools.partial(gradient_kernel, order), out_shape=membe...  2.88 us
    ppermute x3, starting transfers between devices, shards(): link_halo = lax.ppermute(half, 'cell', link_pairs)  2 us
  transfers between devices with their start and end apart: 12, of which 9 were waited for; matrix products, arithmetic and copies ran while one was open for 0% of the time, Pallas kernels for 3%

commit v1 on v0

--- a/solution.py
+++ b/solution.py
@@ -32,23 +32,29 @@
         self.owned = ray_blocks // count
         self.half_blocks = ray_blocks // 2
         self.upper = count // 4
-        self.ring = [chip + side * self.upper for chip in range(self.upper) for side in range(2)]
+        self.rings = (
+            [chip + side * self.upper for chip in range(self.upper) for side in range(2)],
+            list(range(count // 2)),
+        )
 
     def core(self):
         return lax.rem(lax.axis_index("cell"), 2)
 
     def place(self, core, q):
         owner = lax.div(q, self.owned)
+        owner_core = lax.rem(owner, 2)
         other_core = lax.rem(owner + core, 2)
         chip = lax.div(owner, 2)
-        position = 2 * lax.rem(chip, self.upper) + lax.div(chip, self.upper)
+        alternating = 2 * lax.rem(chip, self.upper) + lax.div(chip, self.upper)
+        position = jnp.where(owner_core == 0, alternating, chip)
         return other_core * self.half_blocks + position * self.owned + lax.rem(q, self.owned)
 
     def survey(self, core, survey_ref, i):
         other_core, rest = divmod(i, self.half_blocks)
         position, offset = divmod(rest, self.owned)
-        owner = 2 * self.ring[position] + (1 - core if other_core else core)
-        return survey_ref[owner * self.owned + offset]
+        owner_core = 1 - core if other_core else core
+        chip = jnp.where(owner_core == 0, self.rings[0][position], self.rings[1][position])
+        return survey_ref[(2 * chip + owner_core) * self.owned + offset]
 
 
 def forward(order, survey_ref, half_ref, dense_ref, own_ref, away_ref):
@@ -227,7 +233,7 @@
 
     chip_pairs = [(i, i ^ 1) for i in range(count)]
     link_pairs = [pair for i in range(1, count - 1, 2) for pair in ((i, i + 1), (i + 1, i))]
-    same_core = [[2 * chip + core for chip in order.ring] for core in range(2)]
+    same_core = [[2 * chip + core for chip in ring] for core, ring in enumerate(order.rings)]
 
     def exchange(array):
         return lax.all_to_all(

time: 86.2 us -> 86.2 us (level)
  no operation moved by 1% of the time
where the time goes in v1:
time: 86.2 us; the launch traced here: 85.8 us
  blocking collectives  66.6 us (77%)
  Pallas kernels  10.4 us (12%)
  starting transfers between devices  3.75 us (4%)
  waiting for transfers between devices  3.36 us (4%)
  between operations  1.49 us (2%)
    all_to_all x6, blocking collectives, exchange(): lax.all_to_all(array, 'cell', split_axis=0, concat_axis=0, axis_index_gro...  66.6 us
    pallas_call x3, Pallas kernels, shards(): pl.pallas_call(functools.partial(last_kernel if last else step_kernel, or...  4.36 us
    pallas_call x1, Pallas kernels, shards(): pl.pallas_call(functools.partial(setup_kernel, order), out_shape=(bf16(ra...  3.05 us
    pallas_call x3, Pallas kernels, shards(): pl.pallas_call(functools.partial(gradient_kernel, order), out_shape=membe...  2.89 us
    ppermute x3, starting transfers between devices, shards(): link_halo = lax.ppermute(half, 'cell', link_pairs)  2 us
  transfers between devices with their start and end apart: 12, of which 9 were waited for; matrix products, arithmetic and copies ran while one was open for 0% of the time, Pallas kernels for 3%

profile of v1, /device:TPU:0, one launch (start us, length us, event | category | flops | bytes accessed | tf_op | source)
XLA Modules:
  0.0 85.8 jit_solution(4246884772444439020)
XLA Ops:
  1.3 3.0 %shard_map.95 = (bf16[16,128,256]{2,1,0:T(8,128)(2,1)S(1)}, bf16[8,64,256]{2,1,0:T(8,128)(2,1)S(1)}, f32[8,64,128]{2,1,0:T(8,128)S(1)}, f32[8,64,128]{2,1,0:T(8,128)S(1)}) custom-call(s32[1]{0:T(128)S(6)} %copy.10.count_ref, s32[64]{0:T(128)} %ray_hbm.1, s32[64]{0:T(128)} %cell_hbm.1, s32[16]{0:T(128)} %survey_ref.11, f32[8,64,256]{2,1,0:T(8,128)} %prior_ref.5, ...), custom_call_target="tpu_custom_call" | custom-call | tf_op jit(solution)/shard_map/pallas_call | solution.py:216
  4.4 0.5 collective-permute-start
  4.9 0.1 collective-permute-start.1
  5.0 0.7 collective-permute-start.2
  5.7 0.4 collective-permute-done
  6.1 0.4 collective-permute-done.1.chip_ref
  6.5 15.4 %all_to_all.30 = f16[8,64,128]{2,1,0:T(8,128)(2,1)S(1)} all-to-all(f16[8,64,128]{2,1,0:T(8,128)(2,1)S(1)} %multiply_convert_fusion.2), channel_id=1, replica_groups={{0,8,2,10,4,12,6,14},{1,3,5,7,9,11,13,15},{16,24,18,26,20,28,22,30},{17..., dimensions={0} | all-to-all | bytes 262144 | tf_op jit(solution)/shard_map/all_to_all | solution.py:239
  21.8 0.0 collective-permute-done.2.halo_ref.link_ref
  21.9 9.9 %all_to_all.31.residual_ref = bf16[8,64,128]{2,1,0:T(8,128)(2,1)S(1)} all-to-all(bf16[8,64,128]{2,1,0:T(8,128)(2,1)S(1)} %bitcast.9), channel_id=1, replica_groups={{0,8,2,10,4,12,6,14},{1,3,5,7,9,11,13,15},{16,24,18,26,20,28,22,30},{17..., dimensions={0} | all-to-all | bytes 262144 | tf_op jit(solution)/shard_map/all_to_all | solution.py:239
  31.8 1.0 %shard_map.98.partial_ref = f32[8,64,256]{2,1,0:T(8,128)S(1)} custom-call(s32[16]{0:T(128)S(1)} %copy-done.2, bf16[8,64,128]{2,1,0:T(8,128)(2,1)S(1)} %all_to_all.31.residual_ref, bf16[16,128,256]{2,1,0:T(8,128)(2,1)S(1)} %get-tuple-element.40.dense_ref, f32[8,64,256]{2,1,0:T(8,128)S(1)} %copy-done, f32[8,64,256]{2,1,0:T(8,128)S(1)} %copy-done, ...), custom_call_target="tpu_custom_call" | custom-call | tf_op jit(solution)/shard_map/pallas_call | solution.py:271
  32.8 0.4 collective-permute-done.3.residual_ref
  33.1 1.3 %shard_map.99 = (f32[8,64,256]{2,1,0:T(8,128)S(1)}, bf16[8,64,256]{2,1,0:T(8,128)(2,1)S(1)}, f32[8,64,128]{2,1,0:T(8,128)S(1)}, f32[8,64,128]{2,1,0:T(8,128)S(1)}) custom-call(s32[16]{0:T(128)S(1)} %copy-done.2, bf16[8,64,128]{2,1,0:T(8,128)(2,1)S(1)} %collective-permute-done.3.residual_ref, bf16[16,128,256]{2,1,0:T(8,128)(2,1)S(1)} %get-tuple-element.40.dense_ref, ...), custom_call_target="tpu_custom_call" | custom-call | tf_op jit(solution)/shard_map/pallas_call | solution.py:280
  34.5 0.2 collective-permute-start.4
  34.7 0.4 collective-permute-start.5
  35.0 0.7 collective-permute-start.6
  35.7 0.4 collective-permute-done.4
  36.1 0.4 collective-permute-done.5.chip_ref
  36.5 10.9 %all_to_all.32 = f16[8,64,128]{2,1,0:T(8,128)(2,1)S(1)} all-to-all(f16[8,64,128]{2,1,0:T(8,128)(2,1)S(1)} %multiply_convert_fusion.1), channel_id=1, replica_groups={{0,8,2,10,4,12,6,14},{1,3,5,7,9,11,13,15},{16,24,18,26,20,28,22,30},{17..., dimensions={0} | all-to-all | bytes 262144 | tf_op jit(solution)/shard_map/all_to_all | solution.py:239
  47.5 9.8 %all_to_all.33.residual_ref = bf16[8,64,128]{2,1,0:T(8,128)(2,1)S(1)} all-to-all(bf16[8,64,128]{2,1,0:T(8,128)(2,1)S(1)} %bitcast.10), channel_id=1, replica_groups={{0,8,2,10,4,12,6,14},{1,3,5,7,9,11,13,15},{16,24,18,26,20,28,22,30},{17..., dimensions={0} | all-to-all | bytes 262144 | tf_op jit(solution)/shard_map/all_to_all | solution.py:239
  57.3 1.0 %shard_map.102.partial_ref = f32[8,64,256]{2,1,0:T(8,128)S(1)} custom-call(s32[16]{0:T(128)S(1)} %copy-done.2, bf16[8,64,128]{2,1,0:T(8,128)(2,1)S(1)} %all_to_all.33.residual_ref, bf16[16,128,256]{2,1,0:T(8,128)(2,1)S(1)} %get-tuple-element.40.dense_ref, f32[8,64,256]{2,1,0:T(8,128)S(1)} %get-tuple-element.50.members_ref, f32[8,64,256]{2,1,0:T(8,128)S(1)} %copy-done, ...), custom_call_target="tpu_custom_call" | custom-call | tf_op jit(solution)/shard_map/pallas_call | solution.py:271
  58.2 0.4 collective-permute-done.7.residual_ref
  58.6 1.3 %shard_map.103 = (f32[8,64,256]{2,1,0:T(8,128)S(1)}, bf16[8,64,256]{2,1,0:T(8,128)(2,1)S(1)}, f32[8,64,128]{2,1,0:T(8,128)S(1)}, f32[8,64,128]{2,1,0:T(8,128)S(1)}) custom-call(s32[16]{0:T(128)S(1)} %copy-done.2, bf16[8,64,128]{2,1,0:T(8,128)(2,1)S(1)} %collective-permute-done.7.residual_ref, bf16[16,128,256]{2,1,0:T(8,128)(2,1)S(1)} %get-tuple-element.40.dense_ref, ...), custom_call_target="tpu_custom_call" | custom-call | tf_op jit(solution)/shard_map/pallas_call | solution.py:280
  59.9 0.2 collective-permute-start.8
  60.1 0.4 collective-permute-start.9
  60.5 0.7 collective-permute-start.10
  61.2 0.4 collective-permute-done.8
  61.5 0.4 collective-permute-done.9.chip_ref
  61.9 10.9 %all_to_all.34 = f16[8,64,128]{2,1,0:T(8,128)(2,1)S(1)} all-to-all(f16[8,64,128]{2,1,0:T(8,128)(2,1)S(1)} %multiply_convert_fusion), channel_id=1, replica_groups={{0,8,2,10,4,12,6,14},{1,3,5,7,9,11,13,15},{16,24,18,26,20,28,22,30},{17..., dimensions={0} | all-to-all | bytes 262144 | tf_op jit(solution)/shard_map/all_to_all | solution.py:239
  72.9 9.8 %all_to_all.35.residual_ref = bf16[8,64,128]{2,1,0:T(8,128)(2,1)S(1)} all-to-all(bf16[8,64,128]{2,1,0:T(8,128)(2,1)S(1)} %bitcast.11), channel_id=1, replica_groups={{0,8,2,10,4,12,6,14},{1,3,5,7,9,11,13,15},{16,24,18,26,20,28,22,30},{17..., dimensions={0} | all-to-all | bytes 262144 | tf_op jit(solution)/shard_map/all_to_all | solution.py:239
  82.7 1.0 %shard_map.106.partial_ref = f32[8,64,256]{2,1,0:T(8,128)S(1)} custom-call(s32[16]{0:T(128)S(1)} %copy-done.2, bf16[8,64,128]{2,1,0:T(8,128)(2,1)S(1)} %all_to_all.35.residual_ref, bf16[16,128,256]{2,1,0:T(8,128)(2,1)S(1)} %get-tuple-element.40.dense_ref, f32[8,64,256]{2,1,0:T(8,128)S(1)} %get-tuple-element.60.members_ref, f32[8,64,256]{2,1,0:T(8,128)S(1)} %copy-done, ...), custom_call_target="tpu_custom_call" | custom-call | tf_op jit(solution)/shard_map/pallas_call | solution.py:271
  83.7 0.4 collective-permute-done.11.residual_ref
  84.1 1.7 %shard_map.107 = (f32[8,64,256]{2,1,0:T(8,128)}, bf16[8,64,256]{2,1,0:T(8,128)(2,1)}) custom-call(s32[16]{0:T(128)S(1)} %copy-done.2, bf16[8,64,128]{2,1,0:T(8,128)(2,1)S(1)} %collective-permute-done.11.residual_ref, bf16[16,128,256]{2,1,0:T(8,128)(2,1)S(1)} %get-tuple-element.40.dense_ref, f32[8,64,256]{2,1,0:T(8,128)S(1)} %shard_map.106.partial_ref, ...), custom_call_target="tpu_custom_call" | custom-call | tf_op jit(solution)/shard_map/pallas_call | solution.py:280
  (28 shorter events, 0.3 us)
Async XLA Ops:
  0.6 21.2 %copy-start.1 = (f32[1,64,128]{2,1,0:T(8,128)S(1)}, f32[1,64,128]{2,1,0:T(8,128)}, u32[]{:S(2)}) copy-start(f32[1,64,128]{2,1,0:T(8,128)} %observed_ref.8) | copy-start | bytes 98308
  0.6 21.3 %copy-start.3 = (f32[1,128]{1,0:T(1,128)S(1)}, f32[1,128]{1,0:T(1,128)}, u32[]{:S(2)}) copy-start(f32[1,128]{1,0:T(1,128)} %noise_ref.5) | copy-start | bytes 1540
  1.3 30.5 %copy-start = (f32[8,64,256]{2,1,0:T(8,128)S(1)}, f32[8,64,256]{2,1,0:T(8,128)}, u32[]{:S(2)}) copy-start(f32[8,64,256]{2,1,0:T(8,128)} %prior_ref.5) | copy-start | bytes 1572868
  1.3 30.5 %copy-start.2 = (s32[16]{0:T(128)S(1)}, s32[16]{0:T(128)}, u32[]{:S(2)}) copy-start(s32[16]{0:T(128)} %survey_ref.11) | copy-start | bytes 196
  4.4 1.7 %collective-permute-start = (f32[8,64,128]{2,1,0:T(8,128)S(1)}, f32[8,64,128]{2,1,0:T(8,128)S(1)}, u32[]{:S(2)}, u32[]{:S(2)}) collective-permute-start(f32[8,64,128]{2,1,0:T(8,128)S(1)} %get-tuple-element.33), channel_id=1, source_target_pairs={{0,1},{1,0},{2,3},{3,2},{4,5},{5,4},{6,7},{7,6},{8,9},{9,8},{10,11... | collective-permute-start | bytes 786440 | tf_op jit(solution)/shard_map/ppermute | solution.py:245
  4.9 1.5 %collective-permute-start.1 = (bf16[8,64,256]{2,1,0:T(8,128)(2,1)S(1)}, bf16[8,64,256]{2,1,0:T(8,128)(2,1)S(1)}, u32[]{:S(2)}, u32[]{:S(2)}) collective-permute-start(bf16[8,64,256]{2,1,0:T(8,128)(2,1)S(1)} %get-tuple-element.34), channel_id=1, source_target_pairs={{0,1},{1,0},{2,3},{3,2},{4,5},{5,4},{6,7},{7,6},{8,9},{9,8},{10,11... | collective-permute-start | bytes 786440 | tf_op jit(solution)/shard_map/ppermute | solution.py:246
  5.0 16.9 %collective-permute-start.2 = (bf16[8,64,256]{2,1,0:T(8,128)(2,1)S(1)}, bf16[8,64,256]{2,1,0:T(8,128)(2,1)S(1)}, u32[]{:S(2)}, u32[]{:S(2)}) collective-permute-start(bf16[8,64,256]{2,1,0:T(8,128)(2,1)S(1)} %get-tuple-element.34), channel_id=1, source_target_pairs={{1,2},{2,1},{3,4},{4,3},{5,6},{6,5},{7,8},{8,7},{9,10},{10,9},{11,... | collective-permute-start | bytes 786440 | tf_op jit(solution)/shard_map/ppermute | solution.py:249
  31.8 1.3 %collective-permute-start.3 = (bf16[8,64,128]{2,1,0:T(8,128)(2,1)S(1)}, bf16[8,64,128]{2,1,0:T(8,128)(2,1)S(1)}, u32[]{:S(2)}, u32[]{:S(2)}) collective-permute-start(bf16[8,64,128]{2,1,0:T(8,128)(2,1)S(1)} %all_to_all.31.residual_ref), channel_id=1, source_target_pairs={{0,1},{1,0},{2,3},{3,2},{4,5},{5,4},{6,7},{7,6},{8,9},{9,8},{10,11... | collective-permute-start | bytes 393224 | tf_op jit(solution)/shard_map/ppermute | solution.py:270
  34.5 1.6 %collective-permute-start.4 = (f32[8,64,128]{2,1,0:T(8,128)S(1)}, f32[8,64,128]{2,1,0:T(8,128)S(1)}, u32[]{:S(2)}, u32[]{:S(2)}) collective-permute-start(f32[8,64,128]{2,1,0:T(8,128)S(1)} %get-tuple-element.43), channel_id=1, source_target_pairs={{0,1},{1,0},{2,3},{3,2},{4,5},{5,4},{6,7},{7,6},{8,9},{9,8},{10,11... | collective-permute-start | bytes 786440 | tf_op jit(solution)/shard_map/ppermute | solution.py:245
  34.7 1.8 %collective-permute-start.5 = (bf16[8,64,256]{2,1,0:T(8,128)(2,1)S(1)}, bf16[8,64,256]{2,1,0:T(8,128)(2,1)S(1)}, u32[]{:S(2)}, u32[]{:S(2)}) collective-permute-start(bf16[8,64,256]{2,1,0:T(8,128)(2,1)S(1)} %get-tuple-element.44), channel_id=1, source_target_pairs={{0,1},{1,0},{2,3},{3,2},{4,5},{5,4},{6,7},{7,6},{8,9},{9,8},{10,11... | collective-permute-start | bytes 786440 | tf_op jit(solution)/shard_map/ppermute | solution.py:246
  35.0 12.4 %collective-permute-start.6 = (bf16[8,64,256]{2,1,0:T(8,128)(2,1)S(1)}, bf16[8,64,256]{2,1,0:T(8,128)(2,1)S(1)}, u32[]{:S(2)}, u32[]{:S(2)}) collective-permute-start(bf16[8,64,256]{2,1,0:T(8,128)(2,1)S(1)} %get-tuple-element.44), channel_id=1, source_target_pairs={{1,2},{2,1},{3,4},{4,3},{5,6},{6,5},{7,8},{8,7},{9,10},{10,9},{11,... | collective-permute-start | bytes 786440 | tf_op jit(solution)/shard_map/ppermute | solution.py:249
  57.3 1.3 %collective-permute-start.7 = (bf16[8,64,128]{2,1,0:T(8,128)(2,1)S(1)}, bf16[8,64,128]{2,1,0:T(8,128)(2,1)S(1)}, u32[]{:S(2)}, u32[]{:S(2)}) collective-permute-start(bf16[8,64,128]{2,1,0:T(8,128)(2,1)S(1)} %all_to_all.33.residual_ref), channel_id=1, source_target_pairs={{0,1},{1,0},{2,3},{3,2},{4,5},{5,4},{6,7},{7,6},{8,9},{9,8},{10,11... | collective-permute-start | bytes 393224 | tf_op jit(solution)/shard_map/ppermute | solution.py:270
  59.9 1.6 %collective-permute-start.8 = (f32[8,64,128]{2,1,0:T(8,128)S(1)}, f32[8,64,128]{2,1,0:T(8,128)S(1)}, u32[]{:S(2)}, u32[]{:S(2)}) collective-permute-start(f32[8,64,128]{2,1,0:T(8,128)S(1)} %get-tuple-element.53), channel_id=1, source_target_pairs={{0,1},{1,0},{2,3},{3,2},{4,5},{5,4},{6,7},{7,6},{8,9},{9,8},{10,11... | collective-permute-start | bytes 786440 | tf_op jit(solution)/shard_map/ppermute | solution.py:245
  60.1 1.8 %collective-permute-start.9 = (bf16[8,64,256]{2,1,0:T(8,128)(2,1)S(1)}, bf16[8,64,256]{2,1,0:T(8,128)(2,1)S(1)}, u32[]{:S(2)}, u32[]{:S(2)}) collective-permute-start(bf16[8,64,256]{2,1,0:T(8,128)(2,1)S(1)} %get-tuple-element.54), channel_id=1, source_target_pairs={{0,1},{1,0},{2,3},{3,2},{4,5},{5,4},{6,7},{7,6},{8,9},{9,8},{10,11... | collective-permute-start | bytes 786440 | tf_op jit(solution)/shard_map/ppermute | solution.py:246
  60.5 12.4 %collective-permute-start.10 = (bf16[8,64,256]{2,1,0:T(8,128)(2,1)S(1)}, bf16[8,64,256]{2,1,0:T(8,128)(2,1)S(1)}, u32[]{:S(2)}, u32[]{:S(2)}) collective-permute-start(bf16[8,64,256]{2,1,0:T(8,128)(2,1)S(1)} %get-tuple-element.54), channel_id=1, source_target_pairs={{1,2},{2,1},{3,4},{4,3},{5,6},{6,5},{7,8},{8,7},{9,10},{10,9},{11,... | collective-permute-start | bytes 786440 | tf_op jit(solution)/shard_map/ppermute | solution.py:249
  82.7 1.3 %collective-permute-start.11 = (bf16[8,64,128]{2,1,0:T(8,128)(2,1)S(1)}, bf16[8,64,128]{2,1,0:T(8,128)(2,1)S(1)}, u32[]{:S(2)}, u32[]{:S(2)}) collective-permute-start(bf16[8,64,128]{2,1,0:T(8,128)(2,1)S(1)} %all_to_all.35.residual_ref), channel_id=1, source_target_pairs={{0,1},{1,0},{2,3},{3,2},{4,5},{5,4},{6,7},{7,6},{8,9},{9,8},{10,11... | collective-permute-start | bytes 393224 | tf_op jit(solution)/shard_map/ppermute | solution.py:270
